TPU v7x, 32 devices: a whole 2x2x4 slice. The times are simulated.
32 devices in a mesh: layer: 8 (over z, x), width: 4 (over y, core).
Axes of the slice: x: 2, y: 2, z: 4, core: 2. Of those that a mesh axis runs over, the one named last changes fastest.
Arguments:
- mlp_inputs: bfloat16 [8, 768, 4096], P('layer', None, 'width'), may hold values from -6 to 6
- mlp_outputs: bfloat16 [8, 768, 4096], P('layer', None, 'width'), may hold values from -6 to 6
- encoders: bfloat16 [8, 4096, 128], P('layer', 'width'), may hold values from -0.09375 to 0.09375
- encoder_bias: float32 [8, 128], P('layer'), may hold values from -0.5 to 0
- decoders: bfloat16 [8, 8, 128, 4096], P('layer', None, None, 'width'), may hold values from -0.1875 to 0.1875
Outputs:
- loss_mean: float32 [], replicated
- grad_encoders: bfloat16 [8, 4096, 128], P('layer', 'width')
- grad_encoder_bias: float32 [8, 128], P('layer')
- grad_decoders: bfloat16 [8, 8, 128, 4096], P('layer', None, None, 'width')
All inputs are finite; a program needn't handle non-finite values.
Results may differ from a plain program's by a relative error of at most 0.0055.
Values may be sent and summed in bfloat16 or wider, within the bound.
A program may use at most 128 MiB of HBM per device.

v0:
```python
import jax
import jax.numpy as jnp
from jax import lax
from jax.sharding import PartitionSpec as P

D = 4096


sparsity = 8.0


def per_device(mlp_inputs, mlp_outputs, encoders, encoder_bias, decoders):
    inputs_here = mlp_inputs[0]
    outputs_here = mlp_outputs[0]
    decoder = decoders[0]
    position_vectors = inputs_here.shape[0]
    layers = lax.axis_size("layer")
    widths = lax.axis_size("width")
    own_layer = lax.axis_index("layer")
    partial_value = jnp.dot(inputs_here, encoders[0], preferred_element_type=jnp.float32)
    potential = lax.psum(partial_value, "width") + encoder_bias[0][None, :]
    nonzero_latents = jnp.maximum(potential, 0.0)
    positive_indicator = nonzero_latents.astype(jnp.bfloat16)[None]

    def allowed(amount, kind):
        return (jnp.arange(amount) <= own_layer).astype(kind)

    selected_entries = lax.all_gather(positive_indicator, "layer", axis=0, tiled=True)
    masked_all = selected_entries * allowed(layers, jnp.bfloat16)[:, None, None]
    rebuilt = jnp.einsum("ltf,lfd->td", masked_all, decoder, preferred_element_type=jnp.float32)
    misfit = rebuilt - outputs_here.astype(jnp.float32)
    signal = (misfit / position_vectors).astype(jnp.bfloat16)
    local_loss = 0.5 * jnp.sum(misfit * misfit) + sparsity * jnp.sum(nonzero_latents) / widths
    loss_mean = lax.psum(local_loss, ("layer", "width")) / (position_vectors * D * layers)
    grad_decoder = jnp.einsum(
        "ltf,td->lfd", masked_all, signal, preferred_element_type=jnp.float32
    ).astype(jnp.bfloat16)
    terms = jnp.einsum("td,lfd->ltf", signal, decoder, preferred_element_type=jnp.float32)
    shares = lax.psum_scatter(
        terms * allowed(1 * lax.axis_size("layer"), jnp.float32)[:, None, None],
        "layer",
        scatter_dimension=0,
        tiled=True,
    )
    feature_grad = lax.psum(shares[0], "width")
    delta = (feature_grad + sparsity / position_vectors) * (potential > 0).astype(jnp.float32)
    grad_encoder = lax.dot_general(
        inputs_here,
        delta.astype(jnp.bfloat16),
        (((0,), (0,)), ((), ())),
        preferred_element_type=jnp.float32,
    ).astype(jnp.bfloat16)
    grad_bias = jnp.sum(delta, axis=0)
    return (loss_mean, grad_encoder[None], grad_bias[None], grad_decoder[None])


def solution(mesh):
    return jax.shard_map(
        per_device,
        mesh=mesh,
        in_specs=(
            P("layer", None, "width"),
            P("layer", None, "width"),
            P("layer", "width", None),
            P("layer", None),
            P("layer", None, None, "width"),
        ),
        out_specs=(
            P(),
            P("layer", "width", None),
            P("layer", None),
            P("layer", None, None, "width"),
        ),
        check_vma=False,
    )
```

profile of v0, /device:TPU:0, one launch (start us, length us, event | category | flops | bytes accessed | tf_op | source)
XLA Modules:
  0.0 272.5 jit_solution(13929747476927751217)
XLA Ops:
  7.2 0.0 copy-start
  7.2 0.0 copy-start.3
  7.2 0.0 all-reduce.3.cloned.1.call-start
  7.2 2.9 %fusion.9 = f32[768,128]{1,0:T(8,128)} fusion(bf16[1,768,1024]{2,1,0:T(8,128)(2,1)} %param.5, bf16[1,1024,128]{2,1,0:T(8,128)(2,1)} %param.7), kind=kOutput, calls=%fused_computation.12 | convolution fusion | flops 201326592 | bytes 2228224 | tf_op jit(solution)/shard_map/dot_general | solution.py:20
  10.1 0.0 all-reduce.3.cloned.1.call-update
  10.1 0.0 all-gather.3.cloned.1.call-start
  10.2 36.1 %all-reduce.3.cloned.1.call-done = f32[768,128]{1,0:T(8,128)} async-done(((f32[768,128]{1,0:T(8,128)}), f32[768,128]{1,0:T(8,128)}) %all-reduce.3.cloned.1.call-update) | async-done | bytes 393232 | tf_op jit(solution)/shard_map/psum | solution.py:21
  46.3 0.0 copy-done.3
  46.3 1.7 maximum_convert_fusion
  48.0 0.0 all-gather.3.cloned.1.call-update
  48.0 0.0 reduce-scatter.2.cloned.1.call-start
  48.1 45.4 %all-gather.3.cloned.1.call-done = bf16[6144,128]{1,0:T(8,128)(2,1)} async-done(((bf16[768,128]{1,0:T(8,128)(2,1)}), bf16[6144,128]{1,0:T(8,128)(2,1)}) %all-gather.3.cloned.1.call-update) | async-done | bytes 1572880 | tf_op jit(solution)/shard_map/all_gather | solution.py:28
  93.5 2.6 copy.9
  96.0 0.0 copy-done
  96.1 0.0 copy-start.4
  96.1 5.0 %multiply_reduce_fusion = (f32[]{:T(128)}, f32[768,1024,1]{1,0,2:T(8,128)S(1)}) fusion(bf16[1,768,1024]{2,1,0:T(8,128)(2,1)} %param.6, bf16[1,8,128,1024]{3,2,1,0:T(8,128)(2,1)S(1)} %copy-done, bf16[8,768,128]{1,2,0:T(8,128)(2,1)} %copy.9, bf16[8]{0:T(256)(128)(2,1)S(1)} %compare_convert_fusion.1), kind=kOutput, calls=%fused_computation.3 | convolution fusion | flops 1614544896 | bytes 8388628 | tf_op jit(solution)/shard_map/ltf,lfd->td/dot_general | solution.py:30
  101.0 0.0 copy-start.5
  101.0 1.7 copy-done.5
  102.7 0.0 copy-done.4
  102.7 3.6 %multiply_bitcast_fusion = f32[8,768,128]{2,1,0:T(8,128)} fusion(bf16[1,8,128,1024]{3,2,1,0:T(8,128)(2,1)S(1)} %copy-done, f32[8]{0:T(128)S(1)} %compare_convert_fusion, f32[768,1024,1]{1,0,2:T(8,128)S(1)} %get-tuple-element.11, bf16[1,768,1024]{2,1,0:T(8,128)(2,1)S(1)} %copy-done.4), kind=kOutput, calls=%fused_computation.1 | convolution fusion | flops 1614544896 | bytes 9961504 | tf_op jit(solution)/shard_map/td,lfd->ltf/dot_general | solution.py:38
  106.3 0.0 copy-start.1
  106.3 0.0 reduce-scatter.2.cloned.1.call-update
  106.3 0.0 all-reduce.5.cloned.1.call-start
  106.4 73.3 %reduce-scatter.2.cloned.1.call-done = f32[1,768,128]{2,1,0:T(8,128)} async-done(((f32[8,768,128]{2,1,0:T(8,128)}), f32[1,768,128]{2,1,0:T(8,128)}) %reduce-scatter.2.cloned.1.call-update) | async-done | bytes 393232 | tf_op jit(solution)/shard_map/reduce_scatter | solution.py:39
  179.7 0.0 all-reduce.5.cloned.1.call-update
  180.4 33.4 %all-reduce.5.cloned.1.call-done = f32[768,128]{1,0:T(8,128)} async-done(((f32[768,128]{1,0:T(8,128)}), f32[768,128]{1,0:T(8,128)}) %all-reduce.5.cloned.1.call-update) | async-done | bytes 393232 | tf_op jit(solution)/shard_map/psum | solution.py:45
  213.8 0.0 copy-done.1
  213.8 1.7 fusion.23
  216.2 0.0 copy-start.2
  216.2 6.0 %convert_bitcast_fusion = bf16[1,8,128,1024]{3,2,1,0:T(8,128)(2,1)} fusion(bf16[8,768,128]{1,2,0:T(8,128)(2,1)} %copy.9, bf16[8]{0:T(256)(128)(2,1)S(1)} %compare_convert_fusion.1, f32[768,1024,1]{1,0,2:T(8,128)} %copy-done.5, bf16[1,768,1024]{2,1,0:T(8,128)(2,1)} %param.6), kind=kOutput, calls=%fused_computation.8 | convolution fusion | flops 1615593472 | bytes 8388624 | tf_op jit(solution)/shard_map/ltf,td->lfd/dot_general | solution.py:35
  222.2 39.3 %psum.22 = f32[]{:T(128)} all-reduce(f32[]{:T(128)S(6)} %add.30), channel_id=1, replica_groups=mesh['layer'=8,'width'=4] {'layer','width'}, use_global_device_ids=true, to_apply=%region_3.0 | all-reduce | flops 1 | bytes 8 | tf_op jit(solution)/shard_map/psum | solution.py:34
  261.5 0.0 copy-done.2
  261.5 1.8 fusion.16
  263.3 0.8 copy.11
  (2 shorter events, 0.0 us)
Async XLA Ops:
  7.2 88.9 %copy-start = (bf16[1,8,128,1024]{3,2,1,0:T(8,128)(2,1)S(1)}, bf16[1,8,128,1024]{3,2,1,0:T(8,128)(2,1)}, u32[]{:S(2)}) copy-start(bf16[1,8,128,1024]{3,2,1,0:T(8,128)(2,1)} %param.9) | copy-start | bytes 6291460
  7.2 39.1 %copy-start.3 = (f32[1,128]{1,0:T(1,128)S(1)}, f32[1,128]{1,0:T(1,128)}, u32[]{:S(2)}) copy-start(f32[1,128]{1,0:T(1,128)} %param.8) | copy-start | bytes 1540
  7.2 39.1 %all-reduce.3.cloned.1.call-start = ((), (), s32[]{:S(2)}) async-start(), calls=%async_computation.1 | async-start | bytes 786432 | tf_op jit(solution)/shard_map/psum | solution.py:21
  10.1 83.3 %all-gather.3.cloned.1.call-start = ((), (), s32[]{:S(2)}) async-start(), calls=%async_computation.4 | async-start | bytes 1769472 | tf_op jit(solution)/shard_map/all_gather | solution.py:28
  48.0 131.7 %reduce-scatter.2.cloned.1.call-start = ((), (), s32[]{:S(2)}) async-start(), calls=%async_computation.2 | async-start | bytes 3538944 | tf_op jit(solution)/shard_map/reduce_scatter | solution.py:39
  96.1 6.6 %copy-start.4 = (bf16[1,768,1024]{2,1,0:T(8,128)(2,1)S(1)}, bf16[1,768,1024]{2,1,0:T(8,128)(2,1)}, u32[]{:S(2)}) copy-start(bf16[1,768,1024]{2,1,0:T(8,128)(2,1)} %param.6) | copy-start | bytes 4718596
  101.0 1.7 copy-start.5
  106.3 107.5 %copy-start.1 = (f32[768,128]{1,0:T(8,128)S(1)}, f32[768,128]{1,0:T(8,128)}, u32[]{:S(2)}) copy-start(f32[768,128]{1,0:T(8,128)} %all-reduce.3.cloned.1.call-done) | copy-start | bytes 1179652
  106.3 107.5 %all-reduce.5.cloned.1.call-start = ((), (), s32[]{:S(2)}) async-start(), calls=%async_computation.3 | async-start | bytes 786432 | tf_op jit(solution)/shard_map/psum | solution.py:45
  216.2 45.3 %copy-start.2 = (f32[768,128]{1,0:T(8,128)S(1)}, f32[768,128]{1,0:T(8,128)}, u32[]{:S(2)}) copy-start(f32[768,128]{1,0:T(8,128)} %all-reduce.5.cloned.1.call-done) | copy-start | bytes 1179652
Sparse Core Ops, SparseCore 0:
  10.9 35.2 all-reduce.2
  49.3 44.1 all-gather.2
  106.4 73.1 reduce-scatter.1
  182.0 31.7 all-reduce.4
where the time goes:
time: 273 us; the launch traced here: 272 us
  waiting for transfers between devices  188 us (69%)
  blocking collectives  39.3 us (14%)
  matrix products  19.3 us (7%)
  between operations  16.9 us (6%)
  local copies, waits for them, and re-layouts  5.1 us (2%)
  other arithmetic  3.43 us (1%)
    reduce_scatter x1, waiting for transfers between devices, per_device(): lax.psum_scatter(terms * allowed(1 * lax.axis_size('layer'), jnp.float32)...  73.3 us
    all_gather x1, waiting for transfers between devices, per_device(): lax.all_gather(positive_indicator, 'layer', axis=0, tiled=True)  45.4 us
    psum x1, blocking collectives, per_device(): lax.psum(local_loss, ('layer', 'width')) / (position_vectors * D * layers)  39.3 us
    psum x1, waiting for transfers between devices, per_device(): potential = lax.psum(partial_value, 'width') + encoder_bias[0][None, :]  36.1 us
    psum x1, waiting for transfers between devices, per_device(): feature_grad = lax.psum(shares[0], 'width')  33.4 us
    dot_general x1, matrix products, per_device(): jnp.einsum('ltf,td->lfd', masked_all, signal, preferred_element_type=jnp....  6.02 us
  transfers between devices with their start and end apart: 4, of which 4 were waited for; matrix products, arithmetic and copies ran while one was open for 0% of the time, Pallas kernels for 0%

commit v1 on v0

v1 whole, which is shorter than its diff:
```python
import functools

import jax
import jax.numpy as jnp
from jax import lax
from jax.experimental import pallas as pl
from jax.experimental.pallas import tpu as pltpu
from jax.sharding import PartitionSpec as P

SPARSITY = 8.0
MESH = pl.DeviceIdType.MESH
F32 = jnp.float32
BF16 = jnp.bfloat16


def dot_nn(a, b):
    return jnp.dot(a, b, preferred_element_type=F32)


def dot_nt(a, b):
    return lax.dot_general(a, b, (((1,), (1,)), ((), ())), preferred_element_type=F32)


def kernel(
    layers, widths,
    x_hbm, t_hbm, e_hbm, b_ref, d_hbm,
    loss_ref, ge_ref, gb_ref, gd_hbm,
    x, xt, t, enc, dec, acc, sig, fire, fire_t, pot,
    ea_send, ea_recv, ey_send, ey_recv,
    c_send, c_recv, c_own, cy_send, cy_recv, cd_send, cd_recv, fg,
    delta, gb_all, loss_w, loss_l, gd, zero,
    in_sems, x_sems, out_sems, ea_s, ea_r, ey_s, ey_r,
    fd_s, fd_r, fy_s, fy_r, fs_s, fs_r, ff_s, ff_r,
    cs_s, cs_r, cy_s, cy_r, cd_s, cd_r,
    dl_s, dl_r, gb_s, gb_r, lw_s, lw_r, ll_s, ll_r,
):
    tokens, depth = x.shape
    lat = enc.shape[1]
    half, quarter = tokens // 2, tokens // 4
    me = lax.axis_index("layer")
    w = lax.axis_index("width")
    core, y = lax.rem(w, 2), lax.div(w, 2)
    sib = (me, w + 1 - 2 * core)
    ynb = (me, w + 2 - 4 * y)

    def rows(c_at, y_at):
        return pl.ds(pl.multiple_of(c_at * half + y_at * quarter, 16), quarter)

    def remote(src, dst, send_sem, recv_sem, where):
        return pltpu.make_async_remote_copy(
            src_ref=src, dst_ref=dst, send_sem=send_sem, recv_sem=recv_sem,
            device_id=where, device_id_type=MESH,
        )

    own_rows = rows(core, y)
    ynb_rows = rows(core, 1 - y)
    sib_rows = rows(1 - core, y)
    diag_rows = rows(1 - core, 1 - y)

    order = (diag_rows, sib_rows, ynb_rows, own_rows)
    cp_enc = pltpu.make_async_copy(e_hbm.at[0], enc, in_sems.at[0])
    cp_enc.start()
    cp_x = [pltpu.make_async_copy(x_hbm.at[0, r], x.at[r], x_sems.at[k]) for k, r in enumerate(order)]
    for cp in cp_x:
        cp.start()
    cp_t = pltpu.make_async_copy(t_hbm.at[0], t, in_sems.at[1])
    cp_t.start()
    cp_dec = pltpu.make_async_copy(d_hbm.at[0], dec, in_sems.at[2])
    cp_dec.start()

    barrier = pltpu.get_barrier_semaphore()

    def greet_layer(k, carry):
        pl.semaphore_signal(barrier, inc=1, device_id=(lax.rem(me + k, layers), w), device_id_type=MESH)
        return carry

    def greet_width(k, carry):
        pl.semaphore_signal(barrier, inc=1, device_id=(me, lax.rem(w + k, widths)), device_id_type=MESH)
        return carry

    lax.fori_loop(1, layers, greet_layer, 0)
    lax.fori_loop(1, widths, greet_width, 0)

    cp_enc.wait()
    cp_ea = [remote(ea_send.at[k], ea_recv.at[k], ea_s.at[k], ea_r.at[k], sib) for k in range(2)]
    for k in range(2):
        cp_x[k].wait()
        ea_send[k] = dot_nn(x[order[k], :], enc[...])
        if k == 0:
            pl.semaphore_wait(barrier, layers - 1 + widths - 1)
        cp_ea[k].start()
    cp_x[2].wait()
    part = dot_nn(x[ynb_rows, :], enc[...])
    cp_ea[0].wait_recv()
    ey_send[...] = part + ea_recv[0]
    cp_ey = remote(ey_send, ey_recv, ey_s.at[0], ey_r.at[0], ynb)
    cp_ey.start()
    cp_x[3].wait()
    part = dot_nn(x[own_rows, :], enc[...])
    cp_ea[1].wait_recv()
    part = part + ea_recv[1]
    cp_ey.wait_recv()
    potential = part + ey_recv[...] + b_ref[...]
    pot[...] = potential
    active = jnp.maximum(potential, 0.0)
    fire[me, own_rows, :] = active.astype(BF16)
    active_sum = jnp.sum(active.reshape(quarter // 8, 8, lat), axis=0)

    pair = lax.div(me, 2)

    @pl.when(lax.rem(me, 2) == 0)
    def _():
        fire[me + 1, own_rows, :] = jnp.zeros((quarter, lat), BF16)

    def fire_copy(src_layer, dst_layer):
        ref = fire.at[src_layer, own_rows, :]
        return remote(ref, ref, fd_s.at[dst_layer], fd_r.at[src_layer], (dst_layer, w))

    def send_fire(m, carry):
        fire_copy(me, m).start()
        return carry

    lax.fori_loop(me + 1, layers, send_fire, 0)

    def fire_pair(p, r, send, recv, where):
        ref = fire.at[pl.ds(2 * p, 2), r, :]
        return remote(ref, ref, send.at[p], recv.at[p], where)

    zero[...] = jnp.zeros(zero.shape, BF16)

    def zero_copy(p):
        return pltpu.make_async_copy(zero, gd_hbm.at[0, pl.ds(2 * p, 2)], out_sems.at[p])

    def send_zero(p, carry):
        zero_copy(p).start()
        return carry

    lax.fori_loop(pair + 1, layers // 2, send_zero, 0)

    def stage_far(p):
        for j in range(2):
            @pl.when(2 * p + j < me)
            def _():
                fire_copy(2 * p + j, me).wait_recv()
        fire_pair(p, own_rows, fy_s, fy_r, ynb).start()
        fire_pair(p, own_rows, fs_s, fs_r, sib).start()

    def stage_y(p):
        fire_pair(p, ynb_rows, fy_s, fy_r, ynb).wait_recv()
        fire_pair(p, ynb_rows, ff_s, ff_r, sib).start()

    cp_t.wait()
    blk = 128 if tokens % 128 == 0 else 16

    def prepare(k, carry):
        r = pl.ds(pl.multiple_of(k * blk, blk), blk)
        acc[r, :] = -t[r, :].astype(F32)
        return carry

    lax.fori_loop(0, tokens // blk, prepare, 0)

    @pl.when(lax.rem(me, 2) == 0)
    def _():
        stage_far(pair)

    for k in range(0, depth, 256):
        xt[k:k + 256, :] = x[:, k:k + 256].T
    cp_dec.wait()

    cols = 512 if depth % 512 == 0 else 128

    def features(p):
        return jnp.concatenate([fire[2 * p], fire[2 * p + 1]], axis=-1)

    def weights(p, at):
        return dec[pl.ds(2 * p, 2), :, at].reshape(2 * lat, -1)

    def forward(i, carry):
        @pl.when((i <= pair) & ((i > 0) | (lax.rem(me, 2) == 1)))
        def _():
            stage_far(pair - i)

        @pl.when((i >= 1) & (i <= pair + 1))
        def _():
            stage_y(pair - i + 1)

        @pl.when(i >= 2)
        def _():
            p = pair - i + 2
            fire_pair(p, sib_rows, fs_s, fs_r, sib).wait_recv()
            fire_pair(p, diag_rows, ff_s, ff_r, sib).wait_recv()
            f = features(p)
            for n in range(0, depth, cols):
                at = slice(n, n + cols)
                acc[:, at] += dot_nn(f, weights(p, at))
            fire_t[p] = f.T
        return carry

    lax.fori_loop(0, pair + 3, forward, 0)

    def finish(k, total):
        r = pl.ds(pl.multiple_of(k * blk, blk), blk)
        m = acc[r, :]
        sig[r, :] = (m * (1.0 / tokens)).astype(BF16)
        sq = jnp.sum((m * m).reshape(blk // 8, 8, depth), axis=0)
        return total + sum(sq[:, n:n + lat] for n in range(0, depth, lat))

    squares = lax.fori_loop(0, tokens // blk, finish, jnp.zeros((8, lat), F32))
    loss_w[w] = 0.5 * squares + SPARSITY * active_sum

    def width_copy(ref, send, recv, src, dst):
        return remote(ref.at[src], ref.at[src], send.at[dst], recv.at[src], (me, dst))

    for k in range(1, widths):
        width_copy(loss_w, lw_s, lw_r, w, lax.rem(w + k, widths)).start()

    own_half = pl.ds(pl.multiple_of(core * half, 16), half)
    sib_half = pl.ds(pl.multiple_of((1 - core) * half, 16), half)
    keep = pl.ds(pl.multiple_of(y * quarter, 16), quarter)
    give = pl.ds(pl.multiple_of((1 - y) * quarter, 16), quarter)

    def c_copy(p):
        return remote(c_send.at[p], c_recv.at[p], cs_s.at[p], cs_r.at[p], sib)

    def cy_copy(p):
        return remote(cy_send.at[p], cy_recv.at[p], cy_s.at[p], cy_r.at[p], ynb)

    def cd_copy(src_layer, dst_layer):
        return remote(
            cd_send.at[dst_layer], cd_recv.at[src_layer], cd_s.at[dst_layer], cd_r.at[src_layer], (dst_layer, w)
        )

    def gd_copy(p):
        return pltpu.make_async_copy(gd.at[pl.ds(2 * p, 2)], gd_hbm.at[0, pl.ds(2 * p, 2)], out_sems.at[p])

    every = slice(0, depth)

    def backward(i, carry):
        @pl.when(i <= pair)
        def _():
            p = i
            out = dot_nt(sig[sib_half, :], weights(p, every)).astype(BF16)
            for j in range(2):
                c_send[p, j] = out[:, j * lat:(j + 1) * lat]
            c_copy(p).start()
            out = dot_nt(sig[own_half, :], weights(p, every))
            for j in range(2):
                c_own[p, j] = out[:, j * lat:(j + 1) * lat]

        @pl.when((i >= 1) & (i <= pair + 1))
        def _():
            p = i - 1
            c_copy(p).wait_recv()
            for j in range(2):
                cy_send[p, j] = (c_own[p, j, give, :] + c_recv[p, j, give, :].astype(F32)).astype(BF16)
            cy_copy(p).start()

        @pl.when(i <= pair)
        def _():
            p = i
            for n in range(0, depth, cols):
                at = slice(n, n + cols)
                gd[pl.ds(2 * p, 2), :, at] = dot_nn(fire_t[p], sig[:, at]).astype(BF16).reshape(2, lat, cols)
            gd_copy(p).start()

        @pl.when(i >= 2)
        def _():
            p = i - 2
            cy_copy(p).wait_recv()
            for j in range(2):
                l = 2 * p + j
                total = c_own[p, j, keep, :] + c_recv[p, j, keep, :].astype(F32) + cy_recv[p, j].astype(F32)

                @pl.when(l < me)
                def _():
                    cd_send[l] = total.astype(BF16)
                    cd_copy(me, l).start()

                @pl.when(l == me)
                def _():
                    fg[...] = total
        return carry

    lax.fori_loop(0, pair + 3, backward, 0)

    for k in range(1, widths):
        width_copy(loss_w, lw_s, lw_r, lax.rem(w + k, widths), w).wait_recv()
    total = loss_w[0]
    for k in range(1, widths):
        total = total + loss_w[k]
    loss_l[me] = total

    def layer_copy(src, dst):
        return remote(loss_l.at[src], loss_l.at[src], ll_s.at[dst], ll_r.at[src], (dst, w))

    def send_loss(k, carry):
        layer_copy(me, lax.rem(me + k, layers)).start()
        return carry

    lax.fori_loop(1, layers, send_loss, 0)

    def gather(m, carry):
        cd_copy(m, me).wait_recv()
        fg[...] += cd_recv[m].astype(F32)
        return carry

    lax.fori_loop(me + 1, layers, gather, 0)

    d = jnp.where(pot[...] > 0, fg[...] + SPARSITY / tokens, 0.0)
    delta[own_rows, :] = d.astype(BF16)

    def delta_copy(r, k, where):
        return remote(delta.at[r, :], delta.at[r, :], dl_s.at[k], dl_r.at[k], where)

    delta_copy(own_rows, 0, ynb).start()
    delta_copy(own_rows, 1, sib).start()
    gb_all[w] = jnp.sum(d.reshape(quarter // 8, 8, lat), axis=0)
    for k in range(1, widths):
        width_copy(gb_all, gb_s, gb_r, w, lax.rem(w + k, widths)).start()
    delta_copy(ynb_rows, 0, ynb).wait_recv()
    delta_copy(ynb_rows, 2, sib).start()

    def take_loss(k, carry):
        layer_copy(lax.rem(me + k, layers), me).wait_recv()
        return carry

    lax.fori_loop(1, layers, take_loss, 0)
    loss = lax.fori_loop(0, layers, lambda k, s: s + loss_l[k], jnp.zeros((8, lat), F32))
    loss_ref[0, 0] = jnp.sum(loss) / (tokens * depth * widths * layers)

    delta_copy(sib_rows, 1, sib).wait_recv()
    delta_copy(diag_rows, 2, sib).wait_recv()
    ge_ref[0] = dot_nn(xt[...], delta[...]).astype(BF16)
    for k in range(1, widths):
        width_copy(gb_all, gb_s, gb_r, lax.rem(w + k, widths), w).wait_recv()
    bias = gb_all[0]
    for k in range(1, widths):
        bias = bias + gb_all[k]
    gb_ref[...] = jnp.sum(bias, axis=0, keepdims=True)

    for cp in cp_ea:
        cp.wait_send()
    cp_ey.wait_send()

    def drain_fire(m, carry):
        fire_copy(me, m).wait_send()
        return carry

    lax.fori_loop(me + 1, layers, drain_fire, 0)

    def drain_pair(p, carry):
        fire_pair(p, own_rows, fy_s, fy_r, ynb).wait_send()
        fire_pair(p, own_rows, fs_s, fs_r, sib).wait_send()
        fire_pair(p, ynb_rows, ff_s, ff_r, sib).wait_send()
        c_copy(p).wait_send()
        cy_copy(p).wait_send()
        gd_copy(p).wait()
        return carry

    lax.fori_loop(0, pair + 1, drain_pair, 0)

    def drain_zero(p, carry):
        zero_copy(p).wait()
        return carry

    lax.fori_loop(pair + 1, layers // 2, drain_zero, 0)

    def drain_grad(l, carry):
        cd_copy(me, l).wait_send()
        return carry

    lax.fori_loop(0, me, drain_grad, 0)

    def drain_loss(k, carry):
        layer_copy(me, lax.rem(me + k, layers)).wait_send()
        return carry

    lax.fori_loop(1, layers, drain_loss, 0)
    for k in range(1, widths):
        other = lax.rem(w + k, widths)
        width_copy(loss_w, lw_s, lw_r, w, other).wait_send()
        width_copy(gb_all, gb_s, gb_r, w, other).wait_send()
    delta_copy(own_rows, 0, ynb).wait_send()
    delta_copy(own_rows, 1, sib).wait_send()
    delta_copy(ynb_rows, 2, sib).wait_send()


def per_device(x, t, e, b, d):
    layers, widths = lax.axis_size("layer"), lax.axis_size("width")
    tokens, depth = x.shape[1:]
    lat = e.shape[2]
    half, quarter = tokens // 2, tokens // 4
    pairs = layers // 2
    vmem = pltpu.VMEM
    sem = pltpu.SemaphoreType.DMA
    scratch = [
        vmem((tokens, depth), BF16),
        vmem((depth, tokens), BF16),
        vmem((tokens, depth), BF16),
        vmem((depth, lat), BF16),
        vmem((layers, lat, depth), BF16),
        vmem((tokens, depth), F32),
        vmem((tokens, depth), BF16),
        vmem((layers, tokens, lat), BF16),
        vmem((pairs, 2 * lat, tokens), BF16),
        vmem((quarter, lat), F32),
        vmem((2, quarter, lat), F32),
        vmem((2, quarter, lat), F32),
        vmem((quarter, lat), F32),
        vmem((quarter, lat), F32),
        vmem((pairs, 2, half, lat), BF16),
        vmem((pairs, 2, half, lat), BF16),
        vmem((pairs, 2, half, lat), F32),
        vmem((pairs, 2, quarter, lat), BF16),
        vmem((pairs, 2, quarter, lat), BF16),
        vmem((layers, quarter, lat), BF16),
        vmem((layers, quarter, lat), BF16),
        vmem((quarter, lat), F32),
        vmem((tokens, lat), BF16),
        vmem((widths, 8, lat), F32),
        vmem((widths, 8, lat), F32),
        vmem((layers, 8, lat), F32),
        vmem((layers, lat, depth), BF16),
        vmem((2, lat, depth), BF16),
    ]
    scratch += [
        sem((3,)), sem((4,)), sem((pairs,)), sem((2,)), sem((2,)), sem((1,)), sem((1,)),
        sem((layers,)), sem((layers,)), sem((pairs,)), sem((pairs,)),
        sem((pairs,)), sem((pairs,)), sem((pairs,)), sem((pairs,)),
        sem((pairs,)), sem((pairs,)), sem((pairs,)), sem((pairs,)), sem((layers,)), sem((layers,)),
        sem((3,)), sem((3,)), sem((widths,)), sem((widths,)), sem((widths,)), sem((widths,)),
        sem((layers,)), sem((layers,)),
    ]
    anyspace = pl.BlockSpec(memory_space=pl.ANY)
    vspace = pl.BlockSpec(memory_space=pltpu.VMEM)
    loss, ge, gb, gd = pl.pallas_call(
        functools.partial(kernel, layers, widths),
        out_shape=(
            jax.ShapeDtypeStruct((1, 1), F32),
            jax.ShapeDtypeStruct((1, depth, lat), BF16),
            jax.ShapeDtypeStruct((1, lat), F32),
            jax.ShapeDtypeStruct((1, layers, lat, depth), BF16),
        ),
        in_specs=[anyspace, anyspace, anyspace, vspace, anyspace],
        out_specs=(pl.BlockSpec(memory_space=pltpu.SMEM), vspace, vspace, anyspace),
        scratch_shapes=scratch,
        compiler_params=pltpu.CompilerParams(
            collective_id=0, has_side_effects=True, vmem_limit_bytes=60 * 1024 * 1024
        ),
        cost_estimate=pl.CostEstimate(
            flops=6 * tokens * depth * layers * lat, bytes_accessed=4 * layers * lat * depth, transcendentals=0
        ),
    )(x, t, e, b, d)
    return loss.reshape(()), ge, gb, gd


def solution(mesh):
    return jax.shard_map(
        per_device,
        mesh=mesh,
        in_specs=(
            P("layer", None, "width"),
            P("layer", None, "width"),
            P("layer", "width", None),
            P("layer", None),
            P("layer", None, None, "width"),
        ),
        out_specs=(
            P(),
            P("layer", "width", None),
            P("layer", None),
            P("layer", None, None, "width"),
        ),
        check_vma=False,
    )
```

time: 273 us -> 61.1 us (0.22)
  waiting for transfers between devices: 188 us -> 0 us
  Pallas kernels: 0 us -> 51.7 us
  blocking collectives: 39.3 us -> 0 us
  matrix products: 19.3 us -> 0 us
  between operations: 16.9 us -> 2.39 us
  other arithmetic: 3.43 us -> 0 us
    reduce_scatter x1 -> x0, waiting for transfers between devices: 73.3 us -> none  [per_device(): lax.psum_scatter(terms * allowed(1 * lax.axis_size('layer'), jnp.float32)...]
    psum x2 -> x0, waiting for transfers between devices: 69.5 us -> none  [the longest x1 36.1 us: per_device(): potential = lax.psum(partial_value, 'width') + encoder_bias[0][None, :]]
    pallas_call x0 -> x1, Pallas kernels: none -> 51.7 us  [per_device(): pl.pallas_call(functools.partial(kernel, layers, widths), out_shape=(jax....]
    all_gather x1 -> x0, waiting for transfers between devices: 45.4 us -> none  [per_device(): lax.all_gather(positive_indicator, 'layer', axis=0, tiled=True)]
    psum x1 -> x0, blocking collectives: 39.3 us -> none  [per_device(): lax.psum(local_loss, ('layer', 'width')) / (position_vectors * D * layers)]
    dot_general x5 -> x0, matrix products: 19.3 us -> none  [the longest x1 6.02 us: per_device(): jnp.einsum('ltf,td->lfd', masked_all, signal, preferred_element_type=jnp....]
    unnamed x13 -> x3, local copies, waits for them, and re-layouts: 2.53 us -> 5.94 us
  transfers between devices with their start and end apart: 4 -> 0, of which waited for: 4 -> 0; matrix products, arithmetic and copies ran while one was open for 0% -> 0% of each run, Pallas kernels for 0% -> 0%
where the time goes in v1:
time: 61.1 us; the launch traced here: 60 us
  Pallas kernels  51.7 us (85%)
  local copies, waits for them, and re-layouts  5.94 us (10%)
  between operations  2.39 us (4%)
    pallas_call x1, Pallas kernels, per_device(): pl.pallas_call(functools.partial(kernel, layers, widths), out_shape=(jax....  51.7 us
    unnamed x3, local copies, waits for them, and re-layouts  5.94 us

profile of v1, /device:TPU:0, one launch (start us, length us, event | category | flops | bytes accessed | tf_op | source)
XLA Modules:
  0.0 60.0 jit_solution(11615615420037732804)
XLA Ops:
  0.6 51.7 %shard_map.84 = (f32[1,1]{1,0:T(1,128)}, bf16[1,1024,128]{2,1,0:T(8,128)(2,1)}, f32[1,128]{1,0:T(1,128)}, bf16[1,8,128,1024]{3,2,1,0:T(8,128)(2,1)}) custom-call(bf16[1,768,1024]{2,1,0:T(8,128)(2,1)} %x_hbm.1, bf16[1,768,1024]{2,1,0:T(8,128)(2,1)} %t_hbm.1, bf16[1,1024,128]{2,1,0:T(8,128)(2,1)} %e_hbm.1, f32[1,128]{1,0:T(1,128)} %b_ref.1, ...), custom_call_target="tpu_custom_call" | custom-call | flops 4831838208 | bytes 4194304 | tf_op jit(solution)/shard_map/pallas_call | solution.py:436
  53.0 1.7 %copy.14 = bf16[1,1024,128]{2,1,0:T(8,128)(2,1)} copy(bf16[1,1024,128]{2,1,0:T(8,128)(2,1)} %get-tuple-element.17) | data formatting | bytes 524288
  54.6 1.2 %copy.15 = f32[1,128]{1,0:T(1,128)} copy(f32[1,128]{1,0:T(1,128)} %get-tuple-element.18) | data formatting | bytes 1024
  55.8 3.1 %copy.16 = bf16[1,8,128,1024]{3,2,1,0:T(8,128)(2,1)} copy(bf16[1,8,128,1024]{3,2,1,0:T(8,128)(2,1)} %get-tuple-element.19) | data formatting | bytes 4194304

commit v2 on v1

--- a/solution.py
+++ b/solution.py
@@ -1,4 +1,5 @@
 import functools
+import math
 
 import jax
 import jax.numpy as jnp
@@ -247,14 +248,18 @@
             for j in range(2):
                 c_own[p, j] = out[:, j * lat:(j + 1) * lat]
 
-        @pl.when((i >= 1) & (i <= pair + 1))
-        def _():
-            p = i - 1
+        @pl.when(i >= 2)
+        def _():
+            p = i - 2
             c_copy(p).wait_recv()
             for j in range(2):
                 cy_send[p, j] = (c_own[p, j, give, :] + c_recv[p, j, give, :].astype(F32)).astype(BF16)
             cy_copy(p).start()
-
+        return carry
+
+    lax.fori_loop(0, pair + 3, backward, 0)
+
+    def outward(i, carry):
         @pl.when(i <= pair)
         def _():
             p = i
@@ -281,7 +286,7 @@
                     fg[...] = total
         return carry
 
-    lax.fori_loop(0, pair + 3, backward, 0)
+    lax.fori_loop(0, pair + 3, outward, 0)
 
     for k in range(1, widths):
         width_copy(loss_w, lw_s, lw_r, lax.rem(w + k, widths), w).wait_recv()
@@ -326,7 +331,7 @@
 
     lax.fori_loop(1, layers, take_loss, 0)
     loss = lax.fori_loop(0, layers, lambda k, s: s + loss_l[k], jnp.zeros((8, lat), F32))
-    loss_ref[0, 0] = jnp.sum(loss) / (tokens * depth * widths * layers)
+    loss_ref[...] = jnp.full((8, lat), jnp.sum(loss) / (tokens * depth * widths * layers), F32)
 
     delta_copy(sib_rows, 1, sib).wait_recv()
     delta_copy(diag_rows, 2, sib).wait_recv()
@@ -383,6 +388,44 @@
     delta_copy(own_rows, 0, ynb).wait_send()
     delta_copy(own_rows, 1, sib).wait_send()
     delta_copy(ynb_rows, 2, sib).wait_send()
+
+
+def copies(cuts, loss_in, ge_in, gb_in, gd_in, loss_out, ge_out, gb_out, gd_out, sems):
+    layers = gd_in.shape[1]
+    moves = [(ge_in, ge_out), (gb_in, gb_out)]
+    for k in range(cuts):
+        at = pl.ds(k * (layers // cuts), layers // cuts)
+        moves.append((gd_in.at[:, at], gd_out.at[:, at]))
+    moves = [pltpu.make_async_copy(a, b, sems.at[k]) for k, (a, b) in enumerate(moves)]
+    for m in moves:
+        m.start()
+    loss_out[0, 0] = loss_in[0, 0]
+    for m in moves:
+        m.wait()
+
+
+def hand_out(loss, ge, gb, gd):
+    cuts = 4
+    anyspace = pl.BlockSpec(memory_space=pl.ANY)
+    smem = pl.BlockSpec(memory_space=pltpu.SMEM)
+    hbm = pl.BlockSpec(memory_space=pltpu.HBM)
+    loss, ge, gb, gd = pl.pallas_call(
+        functools.partial(copies, cuts),
+        out_shape=(
+            jax.ShapeDtypeStruct((1, 1), F32),
+            jax.ShapeDtypeStruct(ge.shape, ge.dtype),
+            jax.ShapeDtypeStruct(gb.shape, gb.dtype),
+            jax.ShapeDtypeStruct(gd.shape, gd.dtype),
+        ),
+        in_specs=[pl.BlockSpec(memory_space=pltpu.VMEM), anyspace, anyspace, anyspace],
+        out_specs=(smem, hbm, hbm, hbm),
+        scratch_shapes=[pltpu.SemaphoreType.DMA((cuts + 2,))],
+        compiler_params=pltpu.CompilerParams(vmem_limit_bytes=2**20),
+        cost_estimate=pl.CostEstimate(
+            flops=0, bytes_accessed=4 * (gd.size + ge.size), transcendentals=0
+        ),
+    )(loss, ge, gb, gd)
+    return loss.reshape(()), ge, gb, gd
 
 
 def per_device(x, t, e, b, d):
@@ -431,27 +474,30 @@
         sem((3,)), sem((3,)), sem((widths,)), sem((widths,)), sem((widths,)), sem((widths,)),
         sem((layers,)), sem((layers,)),
     ]
+    held = sum(math.prod(s.shape) * jnp.dtype(s.dtype).itemsize for s in scratch[:28])
+    limit = max(53, min(60, held // 2**20 + 8)) * 2**20
     anyspace = pl.BlockSpec(memory_space=pl.ANY)
     vspace = pl.BlockSpec(memory_space=pltpu.VMEM)
+    hbm = pl.BlockSpec(memory_space=pltpu.HBM)
     loss, ge, gb, gd = pl.pallas_call(
         functools.partial(kernel, layers, widths),
         out_shape=(
-            jax.ShapeDtypeStruct((1, 1), F32),
+            jax.ShapeDtypeStruct((8, lat), F32),
             jax.ShapeDtypeStruct((1, depth, lat), BF16),
             jax.ShapeDtypeStruct((1, lat), F32),
             jax.ShapeDtypeStruct((1, layers, lat, depth), BF16),
         ),
-        in_specs=[anyspace, anyspace, anyspace, vspace, anyspace],
-        out_specs=(pl.BlockSpec(memory_space=pltpu.SMEM), vspace, vspace, anyspace),
+        in_specs=[hbm, hbm, hbm, vspace, hbm],
+        out_specs=(vspace, vspace, vspace, anyspace),
         scratch_shapes=scratch,
         compiler_params=pltpu.CompilerParams(
-            collective_id=0, has_side_effects=True, vmem_limit_bytes=60 * 1024 * 1024
+            collective_id=0, has_side_effects=True, vmem_limit_bytes=limit
         ),
         cost_estimate=pl.CostEstimate(
             flops=6 * tokens * depth * layers * lat, bytes_accessed=4 * layers * lat * depth, transcendentals=0
         ),
     )(x, t, e, b, d)
-    return loss.reshape(()), ge, gb, gd
+    return hand_out(loss, ge, gb, gd)
 
 
 def solution(mesh):

time: 61.1 us -> 56.3 us (0.921); the launches traced: 60 us -> 56.1 us
  local copies, waits for them, and re-layouts: 5.94 us -> 3.18 us
  between operations: 2.39 us -> 0.66 us
    unnamed x3 -> x6, local copies, waits for them, and re-layouts: 5.94 us -> 3.18 us
    pallas_call x0 -> x1, Pallas kernels: none -> 1.97 us  [hand_out(): pl.pallas_call(functools.partial(copies, cuts), out_shape=(jax.ShapeDtype...]
    pallas_call x1, Pallas kernels: 51.7 us -> 50.3 us  [per_device(): pl.pallas_call(functools.partial(kernel, layers, widths), out_shape=(jax....]
where the time goes in v2:
time: 56.3 us; the launch traced here: 56.1 us
  Pallas kernels  52.3 us (93%)
  local copies, waits for them, and re-layouts  3.18 us (6%)
  between operations  0.66 us (1%)
    pallas_call x1, Pallas kernels, per_device(): pl.pallas_call(functools.partial(kernel, layers, widths), out_shape=(jax....  50.3 us
    unnamed x6, local copies, waits for them, and re-layouts  3.18 us
    pallas_call x1, Pallas kernels, hand_out(): pl.pallas_call(functools.partial(copies, cuts), out_shape=(jax.ShapeDtype...  1.97 us

profile of v2, /device:TPU:0, one launch (start us, length us, event | category | flops | bytes accessed | tf_op | source)
XLA Modules:
  0.0 56.1 jit_solution(12543549830617886284)
XLA Ops:
  0.6 0.0 copy-start.1
  0.6 0.9 %copy-done.1 = bf16[1,1024,128]{2,1,0:T(8,128)(2,1)S(1)} copy-done((bf16[1,1024,128]{2,1,0:T(8,128)(2,1)S(1)}, bf16[1,1024,128]{2,1,0:T(8,128)(2,1)}, u32[]{:S(2)}) %copy-start.1) | copy-done | bytes 262168
  1.6 0.0 copy-start.2
  1.6 0.7 %copy-done.2 = f32[1,128]{1,0:T(1,128)S(1)} copy-done((f32[1,128]{1,0:T(1,128)S(1)}, f32[1,128]{1,0:T(1,128)}, u32[]{:S(2)}) %copy-start.2) | copy-done | bytes 536
  2.2 50.3 %shard_map.84 = (f32[8,128]{1,0:T(8,128)S(1)}, bf16[1,1024,128]{2,1,0:T(8,128)(2,1)S(1)}, f32[1,128]{1,0:T(1,128)S(1)}, bf16[1,8,128,1024]{3,2,1,0:T(8,128)(2,1)}) custom-call(bf16[1,768,1024]{2,1,0:T(8,128)(2,1)} %x_hbm.1, bf16[1,768,1024]{2,1,0:T(8,128)(2,1)} %t_hbm.1, bf16[1,1024,128]{2,1,0:T(8,128)(2,1)S(1)} %copy-done.1, f32[1,128]{1,0:T(1,128)S(1)} %copy-done.2, ...), custom_call_target="tpu_custom_call" | custom-call | flops 4831838208 | bytes 4194304 | tf_op jit(solution)/shard_map/pallas_call | solution.py:482
  52.6 0.0 copy-start
  52.6 1.6 %copy-done = bf16[1,8,128,1024]{3,2,1,0:T(8,128)(2,1)S(1)} copy-done((bf16[1,8,128,1024]{3,2,1,0:T(8,128)(2,1)S(1)}, bf16[1,8,128,1024]{3,2,1,0:T(8,128)(2,1)}, u32[]{:S(2)}) %copy-start) | copy-done | bytes 2097176
  54.2 2.0 %shard_map.85 = (f32[1,1]{1,0:T(1,128)}, bf16[1,1024,128]{2,1,0:T(8,128)(2,1)}, f32[1,128]{1,0:T(1,128)}, bf16[1,8,128,1024]{3,2,1,0:T(8,128)(2,1)}) custom-call(f32[8,128]{1,0:T(8,128)S(1)} %get-tuple-element.12.loss_in, bf16[1,1024,128]{2,1,0:T(8,128)(2,1)S(1)} %get-tuple-element.13.ge_in, f32[1,128]{1,0:T(1,128)S(1)} %get-tuple-element.14.gb_in, ...), custom_call_target="tpu_custom_call" | custom-call | bytes 4718592 | tf_op jit(solution)/shard_map/pallas_call | solution.py:412
Async XLA Ops:
  0.6 1.0 %copy-start.1 = (bf16[1,1024,128]{2,1,0:T(8,128)(2,1)S(1)}, bf16[1,1024,128]{2,1,0:T(8,128)(2,1)}, u32[]{:S(2)}) copy-start(bf16[1,1024,128]{2,1,0:T(8,128)(2,1)} %e_hbm.1) | copy-start | bytes 786436
  1.6 0.7 %copy-start.2 = (f32[1,128]{1,0:T(1,128)S(1)}, f32[1,128]{1,0:T(1,128)}, u32[]{:S(2)}) copy-start(f32[1,128]{1,0:T(1,128)} %b_ref.1) | copy-start | bytes 1540
  52.6 1.6 %copy-start = (bf16[1,8,128,1024]{3,2,1,0:T(8,128)(2,1)S(1)}, bf16[1,8,128,1024]{3,2,1,0:T(8,128)(2,1)}, u32[]{:S(2)}) copy-start(bf16[1,8,128,1024]{3,2,1,0:T(8,128)(2,1)} %get-tuple-element.15.gd_in) | copy-start | bytes 6291460

commit v3 on v2

--- a/solution.py
+++ b/solution.py
@@ -150,6 +150,10 @@
         fire_pair(p, ynb_rows, fy_s, fy_r, ynb).wait_recv()
         fire_pair(p, ynb_rows, ff_s, ff_r, sib).start()
 
+    @pl.when(lax.rem(me, 2) == 0)
+    def _():
+        stage_far(pair)
+
     cp_t.wait()
     blk = 128 if tokens % 128 == 0 else 16
 
@@ -160,12 +164,6 @@
 
     lax.fori_loop(0, tokens // blk, prepare, 0)
 
-    @pl.when(lax.rem(me, 2) == 0)
-    def _():
-        stage_far(pair)
-
-    for k in range(0, depth, 256):
-        xt[k:k + 256, :] = x[:, k:k + 256].T
     cp_dec.wait()
 
     cols = 512 if depth % 512 == 0 else 128
@@ -303,6 +301,9 @@
         return carry
 
     lax.fori_loop(1, layers, send_loss, 0)
+
+    for k in range(0, depth, 256):
+        xt[k:k + 256, :] = x[:, k:k + 256].T
 
     def gather(m, carry):
         cd_copy(m, me).wait_recv()

time: 56.3 us -> 56.3 us (level)
  no operation moved by 1% of the time
where the time goes in v3:
time: 56.3 us; the launch traced here: 56.1 us
  Pallas kernels  52.3 us (93%)
  local copies, waits for them, and re-layouts  3.18 us (6%)
  between operations  0.66 us (1%)
    pallas_call x1, Pallas kernels, per_device(): pl.pallas_call(functools.partial(kernel, layers, widths), out_shape=(jax....  50.3 us
    unnamed x6, local copies, waits for them, and re-layouts  3.18 us
    pallas_call x1, Pallas kernels, hand_out(): pl.pallas_call(functools.partial(copies, cuts), out_shape=(jax.ShapeDtype...  1.97 us

profile of v3, /device:TPU:0, one launch (start us, length us, event | category | flops | bytes accessed | tf_op | source)
XLA Modules:
  0.0 56.1 jit_solution(14786178111499475926)
XLA Ops:
  0.6 0.0 copy-start.1
  0.6 0.9 %copy-done.1 = bf16[1,1024,128]{2,1,0:T(8,128)(2,1)S(1)} copy-done((bf16[1,1024,128]{2,1,0:T(8,128)(2,1)S(1)}, bf16[1,1024,128]{2,1,0:T(8,128)(2,1)}, u32[]{:S(2)}) %copy-start.1) | copy-done | bytes 262168
  1.6 0.0 copy-start.2
  1.6 0.7 %copy-done.2 = f32[1,128]{1,0:T(1,128)S(1)} copy-done((f32[1,128]{1,0:T(1,128)S(1)}, f32[1,128]{1,0:T(1,128)}, u32[]{:S(2)}) %copy-start.2) | copy-done | bytes 536
  2.2 50.3 %shard_map.84 = (f32[8,128]{1,0:T(8,128)S(1)}, bf16[1,1024,128]{2,1,0:T(8,128)(2,1)S(1)}, f32[1,128]{1,0:T(1,128)S(1)}, bf16[1,8,128,1024]{3,2,1,0:T(8,128)(2,1)}) custom-call(bf16[1,768,1024]{2,1,0:T(8,128)(2,1)} %x_hbm.1, bf16[1,768,1024]{2,1,0:T(8,128)(2,1)} %t_hbm.1, bf16[1,1024,128]{2,1,0:T(8,128)(2,1)S(1)} %copy-done.1, f32[1,128]{1,0:T(1,128)S(1)} %copy-done.2, ...), custom_call_target="tpu_custom_call" | custom-call | flops 4831838208 | bytes 4194304 | tf_op jit(solution)/shard_map/pallas_call | solution.py:483
  52.6 0.0 copy-start
  52.6 1.6 %copy-done = bf16[1,8,128,1024]{3,2,1,0:T(8,128)(2,1)S(1)} copy-done((bf16[1,8,128,1024]{3,2,1,0:T(8,128)(2,1)S(1)}, bf16[1,8,128,1024]{3,2,1,0:T(8,128)(2,1)}, u32[]{:S(2)}) %copy-start) | copy-done | bytes 2097176
  54.2 2.0 %shard_map.85 = (f32[1,1]{1,0:T(1,128)}, bf16[1,1024,128]{2,1,0:T(8,128)(2,1)}, f32[1,128]{1,0:T(1,128)}, bf16[1,8,128,1024]{3,2,1,0:T(8,128)(2,1)}) custom-call(f32[8,128]{1,0:T(8,128)S(1)} %get-tuple-element.12.loss_in, bf16[1,1024,128]{2,1,0:T(8,128)(2,1)S(1)} %get-tuple-element.13.ge_in, f32[1,128]{1,0:T(1,128)S(1)} %get-tuple-element.14.gb_in, ...), custom_call_target="tpu_custom_call" | custom-call | bytes 4718592 | tf_op jit(solution)/shard_map/pallas_call | solution.py:413
Async XLA Ops:
  0.6 1.0 %copy-start.1 = (bf16[1,1024,128]{2,1,0:T(8,128)(2,1)S(1)}, bf16[1,1024,128]{2,1,0:T(8,128)(2,1)}, u32[]{:S(2)}) copy-start(bf16[1,1024,128]{2,1,0:T(8,128)(2,1)} %e_hbm.1) | copy-start | bytes 786436
  1.6 0.7 %copy-start.2 = (f32[1,128]{1,0:T(1,128)S(1)}, f32[1,128]{1,0:T(1,128)}, u32[]{:S(2)}) copy-start(f32[1,128]{1,0:T(1,128)} %b_ref.1) | copy-start | bytes 1540
  52.6 1.6 %copy-start = (bf16[1,8,128,1024]{3,2,1,0:T(8,128)(2,1)S(1)}, bf16[1,8,128,1024]{3,2,1,0:T(8,128)(2,1)}, u32[]{:S(2)}) copy-start(bf16[1,8,128,1024]{3,2,1,0:T(8,128)(2,1)} %get-tuple-element.15.gd_in) | copy-start | bytes 6291460
